TPU v7x, 256 devices: a whole 4x4x8 slice. The times are simulated.
256 devices in a mesh: ctx: 4 (over z_hi), tp: 8 (over y, core), dec: 8 (over x, z_lo).
Axes of the slice: x: 4, y: 4, z: 8 (z_hi: 4, z_lo: 2; z = z_hi * 2 + z_lo), core: 2. Of those that a mesh axis runs over, the one named last changes fastest.
Arguments:
- cache: bfloat16 [8, 1024, 576], P('dec', 'ctx'), may hold values from -6 to 6
- lengths: int32 [8], P('dec'), may hold values from 1 to 1024
- slot_sequence: int32 [8], replicated, may hold values from 0 to 7, each once
- parents: int32 [8, 64], P('dec'), may hold values from 0 to 62, as said below
- query_nope: bfloat16 [8, 64, 128, 128], P('dec', None, 'tp'), may hold values from -6 to 6
- query_rope: bfloat16 [8, 64, 128, 64], P('dec', None, 'tp'), may hold values from -90 to 90
- new_latent: bfloat16 [8, 64, 576], P('dec'), may hold values from -6 to 6
- key_up: bfloat16 [128, 128, 512], P('tp'), may hold values from -0.5 to 0.5
- value_up: bfloat16 [128, 512, 128], P('tp'), may hold values from -0.25 to 0.25
- out_proj: bfloat16 [16384, 7168], P('tp', ('ctx', 'dec')), may hold values from -0.046875 to 0.046875
Outputs:
- attended: bfloat16 [8, 64, 7168], P(None, 'tp', ('ctx', 'dec'))
Inputs may be any that keep to these rules, and one draw needn't show every extreme that they name: `slot_sequence`: every sequence is held by exactly one slot. parents[s, 0] = 0 and parents[s, i] < i for every i >= 1.
All inputs are finite; a program needn't handle non-finite values.
Results may differ from a plain program's by a relative error of at most 0.024.
Values may be sent and summed in bfloat16 or wider, within the bound.
A program may use at most 64 MiB of HBM per device.

v0:
```python
import math
import jax
import jax.numpy as jnp
from jax import lax
from jax.sharding import PartitionSpec as P


def joined_along(blocks, dim):
    shape = list(blocks.shape[1:])
    shape[dim] *= blocks.shape[0]
    return jnp.moveaxis(blocks, 0, dim).reshape(shape)


def sent_to_all(value, axis):
    copies = jnp.broadcast_to(value, (lax.axis_size(axis), *value.shape))
    return lax.all_to_all(copies, axis, split_axis=0, concat_axis=0, tiled=True)


def collect(value, axis, dim):
    return joined_along(sent_to_all(value, axis), dim)


def sent_together(arrays, axis, dim, along):
    columns = [a.reshape(*a.shape[:along], -1) for a in arrays]
    both = jnp.concatenate(columns, axis=along)
    whole, at, done = (collect(both, axis, dim), 0, [])
    for a, column in zip(arrays, columns):
        piece = whole[..., at : at + column.shape[along]]
        done.append(piece.reshape(*piece.shape[:along], *a.shape[along:]))
        at += column.shape[along]
    return tuple(done)


def for_sending(value):

    def short(part):
        return part.astype(jnp.bfloat16) if part.dtype == jnp.float32 else part

    return jax.tree.map(short, value)


def in_blocks(value, dim, size):
    before, after = (value.shape[:dim], value.shape[dim + 1 :])
    return jnp.moveaxis(value.reshape(*before, size, -1, *after), dim, 0)


def sent_and_summed(value, axis, dim):
    size = lax.axis_size(axis)
    blocks = lax.all_to_all(in_blocks(value, dim, size), axis, 0, 0, tiled=True)
    return jnp.sum(blocks.astype(jnp.float32), axis=0)


def ancestors(parents):
    node_count = parents.shape[-1]
    node_ids = jnp.arange(node_count, dtype=jnp.int32)
    parent_link = (parents[..., :, None] == node_ids).astype(jnp.float32)
    closure = jnp.maximum(parent_link, jnp.eye(node_count, dtype=jnp.float32))
    for _ in range(node_count.bit_length()):
        closure = jnp.minimum(
            jnp.einsum("sij,sjk->sik", closure, closure, precision=lax.Precision.HIGHEST), 1.0
        )
    return closure


def partial_softmax(queries, key_rows, live_mask, latent, score_scale):
    scores = (
        jnp.einsum("snhc,spc->snhp", queries, key_rows, preferred_element_type=jnp.float32)
        * score_scale
    )
    alive = live_mask > 0
    scores = jnp.where(alive, scores, -1e30)
    row_peak = jnp.max(scores, axis=-1)
    expo = jnp.where(alive, jnp.exp(scores - row_peak[..., None]), 0.0)
    row_total = jnp.sum(expo, axis=-1)
    weighted = jnp.einsum(
        "snhp,spc->snhc",
        expo.astype(jnp.bfloat16),
        key_rows[..., :latent],
        preferred_element_type=jnp.float32,
    )
    return (row_peak, row_total, weighted)


def join_parts(first_part, second_part):
    new_peak = jnp.maximum(first_part[0], second_part[0])
    first_factor = jnp.exp(first_part[0] - new_peak)
    second_factor = jnp.exp(second_part[0] - new_peak)
    row_total = first_part[1] * first_factor + second_part[1] * second_factor
    weighted = first_part[2] * first_factor[..., None] + second_part[2] * second_factor[..., None]
    return (new_peak, row_total, weighted)


def pick_rows(select, pieces):
    flat_rows = pieces.reshape(pieces.shape[0], -1)
    chosen = jnp.dot(select, flat_rows, preferred_element_type=jnp.float32)
    return chosen.reshape((select.shape[0],) + pieces.shape[1:]).astype(pieces.dtype)


def to_values(part, value_weight):
    projected = jnp.einsum("snhc,hcv->snhv", part[2], value_weight, precision=lax.Precision.HIGHEST)
    return (part[0], part[1], projected)


def on_device(
    cache,
    lengths,
    slot_sequence,
    parents,
    query_nope,
    query_rope,
    new_latent,
    key_up,
    value_up,
    out_proj,
):
    seq_dev = cache.shape[0]
    ctx_len = cache.shape[1]
    latent = value_up.shape[1]
    node_count = parents.shape[1]
    ctx_count = lax.axis_size("ctx")
    dec_count = lax.axis_size("dec")
    ctx_at = lax.axis_index("ctx")
    dec_at = lax.axis_index("dec")
    score_scale = 1.0 / math.sqrt(key_up.shape[1] + cache.shape[2] - latent)
    positions = ctx_at * ctx_len + jnp.arange(ctx_len, dtype=jnp.int32)
    valid = (positions[None, :] < lengths[:, None]).astype(jnp.bfloat16)
    tree_local = ancestors(parents).astype(jnp.bfloat16)
    value_weight = value_up.astype(jnp.float32)
    wanted = lax.dynamic_slice_in_dim(slot_sequence, dec_at * seq_dev, seq_dev)
    pieces = sent_together((cache, valid), "dec", 0, 2)
    piece_count = pieces[0].shape[0]
    sources = jnp.arange(piece_count, dtype=jnp.int32)
    select = (wanted[:, None] == sources[None, :]).astype(jnp.bfloat16)
    key_rows = pick_rows(select, pieces[0])
    live_rows = pick_rows(select, pieces[1])
    nope_rows, rope_rows, tree_keys, tree_mask = (query_nope, query_rope, new_latent, tree_local)
    absorbed = jnp.einsum(
        "snhd,hdc->snhc", nope_rows, key_up, preferred_element_type=jnp.float32
    ).astype(jnp.bfloat16)
    queries = jnp.concatenate([absorbed, rope_rows], axis=-1)
    cache_part = partial_softmax(
        queries, key_rows, live_rows[:, None, None, :], latent, score_scale
    )
    cache_part = to_values(cache_part, value_weight)
    node_block = node_count // ctx_count
    first_node = ctx_at * node_block
    stacked = tuple((member[None] for member in cache_part))
    spread = jax.tree.map(
        lambda part, own: part.astype(own.dtype),
        lax.all_to_all(for_sending(stacked), "ctx", split_axis=2, concat_axis=0, tiled=True),
        stacked,
    )
    peak_all = jnp.max(spread[0], axis=0)
    factors = jnp.exp(spread[0] - peak_all[None])
    merged = (
        peak_all,
        jnp.sum(spread[1] * factors, axis=0),
        jnp.sum(spread[2] * factors[..., None], axis=0),
    )
    block_queries = lax.dynamic_slice_in_dim(queries, first_node, node_block, 1)
    block_tree = lax.dynamic_slice_in_dim(tree_mask, first_node, node_block, 1)
    tree_part = partial_softmax(
        block_queries, tree_keys, block_tree[:, :, None, :], latent, score_scale
    )
    tree_part = to_values(tree_part, value_weight)
    final = join_parts(merged, tree_part)
    head_values = (final[2] / final[1][..., None]).astype(jnp.bfloat16)
    head_values = head_values.reshape(seq_dev, node_block, -1)
    projected = jnp.einsum(
        "ksnv,vd->ksnd",
        lax.all_gather(head_values[None], ("ctx", "dec"), axis=0, tiled=True),
        out_proj,
        preferred_element_type=jnp.float32,
    )
    column_count = out_proj.shape[1]
    projected = projected.reshape(ctx_count, dec_count, seq_dev, node_block, column_count)
    projected = projected.transpose(1, 2, 0, 3, 4).reshape(
        dec_count * seq_dev, node_count, column_count
    )
    return sent_and_summed(projected.astype(jnp.bfloat16), "tp", 1).astype(jnp.bfloat16)


def solution(mesh):
    return jax.shard_map(
        on_device,
        mesh=mesh,
        in_specs=(
            P("dec", "ctx", None),
            P("dec"),
            P(),
            P("dec", None),
            P("dec", None, "tp", None),
            P("dec", None, "tp", None),
            P("dec", None, None),
            P("tp", None, None),
            P("tp", None, None),
            P("tp", ("ctx", "dec")),
        ),
        out_specs=P(None, "tp", ("ctx", "dec")),
        check_vma=False,
    )
```

profile of v0, /device:TPU:1, one launch (start us, length us, event | category | flops | bytes accessed | tf_op | source)
XLA Modules:
  0.0 289.7 jit_solution(6729289213615725984)
XLA Ops:
  7.4 1.0 maximum_bitcast_fusion
  8.3 1.6 broadcast_in_dim.58
  9.9 6.3 %all-to-all-start = ((bf16[8,1,256,577]{2,3,1,0:T(8,128)(2,1)}), bf16[8,1,256,577]{2,3,1,0:T(8,128)(2,1)}, u32[]{:S(2)}, u32[]{:S(2)}) async-start(bf16[8,1,256,577]{2,3,1,0:T(8,128)(2,1)} %broadcast_in_dim.58), calls=%async_computation | async-start | bytes 4784128 | tf_op jit(solution)/shard_map/all_to_all | solution.py:16
  16.5 0.2 convolution_minimum_fusion.5
  16.7 0.2 convolution_minimum_fusion.4
  17.7 1.4 fusion.2
  19.2 0.9 fusion.49
  20.1 0.7 copy.129
  20.8 1.7 fusion.30
  22.5 1.4 copy.136
  23.9 1.3 dynamic_slice.7
  25.1 1.2 bitcast_convert_fusion
  26.3 1.2 fusion.4
  27.5 0.2 fusion.33
  27.7 17.5 %all-to-all-done = bf16[8,1,256,577]{2,3,1,0:T(8,128)(2,1)} async-done(((bf16[8,1,256,577]{2,3,1,0:T(8,128)(2,1)}), bf16[8,1,256,577]{2,3,1,0:T(8,128)(2,1)}, u32[]{:S(2)}, u32[]{:S(2)}) %all-to-all-start) | async-done | bytes 2363424 | tf_op jit(solution)/shard_map/all_to_all | solution.py:16
  45.2 2.2 copy.165
  47.4 0.7 fusion.42
  48.1 1.6 slice.17
  49.7 4.8 %copy.118 = bf16[8,256,576]{2,1,0:T(8,128)(2,1)} copy(bf16[8,256,576]{1,0,2:T(8,128)(2,1)} %slice.17) | data formatting | bytes 4718592 | tf_op jit(solution)/shard_map/slice | solution.py:28
  54.5 5.8 %reshape.529 = bf16[1179648]{0:T(1024)(128)(2,1)} reshape(bf16[8,256,576]{2,1,0:T(8,128)(2,1)} %copy.118) | data formatting | bytes 4718592
  60.4 4.1 %reshape.511 = bf16[8,147456]{1,0:T(8,128)(2,1)} reshape(bf16[1179648]{0:T(1024)(128)(2,1)} %reshape.529) | data formatting | bytes 4718592 | tf_op jit(solution)/shard_map/reshape | solution.py:94
  64.4 4.2 %reshape.531 = bf16[1179648]{0:T(1024)(128)(2,1)} reshape(bf16[8,147456]{1,0:T(8,128)(2,1)} %reshape.511) | data formatting | bytes 4718592
  68.6 5.5 %reshape.532 = bf16[8,256,576]{2,1,0:T(8,128)(2,1)} reshape(bf16[1179648]{0:T(1024)(128)(2,1)} %reshape.531) | data formatting | bytes 4718592
  74.1 2.5 multiply_reduce_fusion
  76.6 2.0 fusion.50
  78.7 1.6 fusion.19
  80.4 0.6 broadcast.166
  81.0 0.8 reduce.17
  81.8 0.7 reshape.533
  82.4 7.7 %all-to-all-start.2 = ((bf16[4,2,128]{2,1,0:T(2,128)(2,1)}), bf16[4,2,128]{2,1,0:T(2,128)(2,1)S(1)}, u32[]{:S(2)}, u32[]{:S(2)}) async-start(bf16[4,2,128]{2,1,0:T(2,128)(2,1)} %reshape.533), calls=%async_computation.2 | async-start | bytes 4096 | tf_op jit(solution)/shard_map/all_to_all | solution.py:150
  90.1 0.4 fusion.22
  90.5 1.1 copy-done.1
  91.7 1.3 fusion.12
  93.2 0.8 reduce.18
  93.9 0.7 reshape.535
  94.6 0.9 copy.122
  95.5 1.1 all-to-all-done.2
  96.6 5.5 %all-to-all-start.3 = ((bf16[4,2,128]{2,1,0:T(2,128)(2,1)}), bf16[4,2,128]{2,1,0:T(2,128)(2,1)S(1)}, u32[]{:S(2)}, u32[]{:S(2)}) async-start(bf16[4,2,128]{2,1,0:T(2,128)(2,1)} %reshape.535), calls=%async_computation.3 | async-start | bytes 4096 | tf_op jit(solution)/shard_map/all_to_all | solution.py:150
  102.5 6.0 %all-to-all-done.3 = bf16[4,2,128]{2,1,0:T(2,128)(2,1)S(1)} async-done(((bf16[4,2,128]{2,1,0:T(2,128)(2,1)}), bf16[4,2,128]{2,1,0:T(2,128)(2,1)S(1)}, u32[]{:S(2)}, u32[]{:S(2)}) %all-to-all-start.3) | async-done | bytes 2080 | tf_op jit(solution)/shard_map/all_to_all | solution.py:150
  108.5 3.4 %all-to-all-start.1 = ((bf16[1,1,64,16,128]{4,3,1,0,2:T(8,128)(2,1)}), bf16[1,1,64,16,128]{4,3,1,0,2:T(8,128)(2,1)S(1)}, u32[]{:S(2)}, u32[]{:S(2)}) async-start(bf16[1,1,64,16,128]{4,3,1,0,2:T(8,128)(2,1)} %copy.122), calls=%async_computation.1 | async-start | bytes 524288 | tf_op jit(solution)/shard_map/all_to_all | solution.py:150
  112.4 7.5 %all-to-all-done.1 = bf16[1,1,64,16,128]{4,3,1,0,2:T(8,128)(2,1)S(1)} async-done(((bf16[1,1,64,16,128]{4,3,1,0,2:T(8,128)(2,1)}), bf16[1,1,64,16,128]{4,3,1,0,2:T(8,128)(2,1)S(1)}, u32[]{:S(2)}, u32[]{:S(2)}) %all-to-all-start.1) | async-done | bytes 262176 | tf_op jit(solution)/shard_map/all_to_all | solution.py:150
  119.9 0.2 fusion.21
  120.1 2.5 fusion.17
  122.7 0.7 broadcast_in_dim_reshape.3
  123.4 126.0 %all-gather.2.cloned.1.call-done = bf16[32,1,16,2048]{3,2,1,0:T(8,128)(2,1)} async-done(((bf16[1,1,16,2048]{3,2,1,0:T(8,128)(2,1)}), bf16[32,1,16,2048]{3,2,1,0:T(8,128)(2,1)}) %all-gather.2.cloned.1.call-update) | async-done | bytes 2097168 | tf_op jit(solution)/shard_map/all_gather | solution.py:171
  249.4 2.5 fusion.9
  252.0 30.2 %all_to_all.40 = bf16[8,8,8,224]{3,2,1,0:T(8,128)(2,1)S(1)} all-to-all(bf16[8,8,8,224]{3,2,1,0:T(8,128)(2,1)S(1)} %copy.139), channel_id=1, replica_groups=mesh['ctx'=4,'tp'=8,'dec'=8] {'tp'}, dimensions={0} | all-to-all | bytes 458752 | tf_op jit(solution)/shard_map/all_to_all | solution.py:49
  282.2 0.7 reduce_sum.55
  (55 shorter events, 2.3 us)
Async XLA Ops:
  6.5 11.2 %copy-start = (bf16[16,128,512]{2,1,0:T(8,128)(2,1)S(1)}, bf16[16,128,512]{2,1,0:T(8,128)(2,1)}, u32[]{:S(2)}) copy-start(bf16[16,128,512]{2,1,0:T(8,128)(2,1)} %param.17) | copy-start | bytes 6291460
  9.9 6.3 %copy-start.3 = (bf16[1,64,16,64]{3,2,1,0:T(8,128)(2,1)S(1)}, bf16[1,64,16,64]{3,2,1,0:T(8,128)(2,1)}, u32[]{:S(2)}) copy-start(bf16[1,64,16,64]{3,2,1,0:T(8,128)(2,1)} %param.15) | copy-start | bytes 393220
  9.9 6.4 %copy-start.9 = (s32[1,64]{1,0:T(1,128)S(1)}, s32[1,64]{1,0:T(1,128)}, u32[]{:S(2)}) copy-start(s32[1,64]{1,0:T(1,128)} %param.13) | copy-start | bytes 772
  9.9 35.3 %all-to-all-start = ((bf16[8,1,256,577]{2,3,1,0:T(8,128)(2,1)}), bf16[8,1,256,577]{2,3,1,0:T(8,128)(2,1)}, u32[]{:S(2)}, u32[]{:S(2)}) async-start(bf16[8,1,256,577]{2,3,1,0:T(8,128)(2,1)} %broadcast_in_dim.58), calls=%async_computation | async-start | bytes 4784128 | tf_op jit(solution)/shard_map/all_to_all | solution.py:16
  17.7 1.5 copy-start.8
  17.7 1.5 copy-start.4
  20.1 0.7 copy-start.7
  68.6 5.5 %copy-start.10 = (f32[8]{0:T(128)S(1)}, f32[8]{0:T(128)}, u32[]{:S(2)}) copy-start(f32[8]{0:T(128)} %bitcast_convert_fusion) | copy-start | bytes 100
  74.1 2.5 copy-start.2
  82.4 14.2 %all-to-all-start.2 = ((bf16[4,2,128]{2,1,0:T(2,128)(2,1)}), bf16[4,2,128]{2,1,0:T(2,128)(2,1)S(1)}, u32[]{:S(2)}, u32[]{:S(2)}) async-start(bf16[4,2,128]{2,1,0:T(2,128)(2,1)} %reshape.533), calls=%async_computation.2 | async-start | bytes 4096 | tf_op jit(solution)/shard_map/all_to_all | solution.py:150
  90.1 1.6 copy-start.1
  91.7 20.7 %copy-start.5 = (f32[16,16]{0,1:T(8,128)S(1)}, f32[16,16]{0,1:T(8,128)}, u32[]{:S(2)}) copy-start(f32[16,16]{0,1:T(8,128)} %copy.129) | copy-start | bytes 3076
  91.7 20.7 %copy-start.6 = (f32[16,16]{0,1:T(8,128)S(1)}, f32[16,16]{0,1:T(8,128)}, u32[]{:S(2)}) copy-start(f32[16,16]{0,1:T(8,128)} %copy.136) | copy-start | bytes 3076
  96.6 11.9 %all-to-all-start.3 = ((bf16[4,2,128]{2,1,0:T(2,128)(2,1)}), bf16[4,2,128]{2,1,0:T(2,128)(2,1)S(1)}, u32[]{:S(2)}, u32[]{:S(2)}) async-start(bf16[4,2,128]{2,1,0:T(2,128)(2,1)} %reshape.535), calls=%async_computation.3 | async-start | bytes 4096 | tf_op jit(solution)/shard_map/all_to_all | solution.py:150
  108.5 11.4 %all-to-all-start.1 = ((bf16[1,1,64,16,128]{4,3,1,0,2:T(8,128)(2,1)}), bf16[1,1,64,16,128]{4,3,1,0,2:T(8,128)(2,1)S(1)}, u32[]{:S(2)}, u32[]{:S(2)}) async-start(bf16[1,1,64,16,128]{4,3,1,0,2:T(8,128)(2,1)} %copy.122), calls=%async_computation.1 | async-start | bytes 524288 | tf_op jit(solution)/shard_map/all_to_all | solution.py:150
  111.9 137.5 %all-gather.2.cloned.1.call-start = ((), (), s32[]{:S(2)}) async-start(), calls=%async_computation.5 | async-start | bytes 2162688 | tf_op jit(solution)/shard_map/all_gather | solution.py:171
Sparse Core Ops, SparseCore 0:
  123.5 125.8 all-gather.1
where the time goes:
time: 291 us; the launch traced here: 290 us
  waiting for transfers between devices  158 us (54%)
  local copies, waits for them, and re-layouts  38.7 us (13%)
  blocking collectives  30.2 us (10%)
  starting transfers between devices  23 us (8%)
  between operations  14.5 us (5%)
  matrix products  13.2 us (5%)
  other arithmetic  12 us (4%)
    all_gather x1, waiting for transfers between devices, on_device(): lax.all_gather(head_values[None], ('ctx', 'dec'), axis=0, tiled=True)  126 us
    all_to_all x1, blocking collectives, sent_and_summed(): blocks = lax.all_to_all(in_blocks(value, dim, size), axis, 0, 0, tiled=True)  30.2 us
    unnamed x31, local copies, waits for them, and re-layouts  18.9 us
    all_to_all x1, waiting for transfers between devices, sent_to_all(): return lax.all_to_all(copies, axis, split_axis=0, concat_axis=0, tiled=True)  17.5 us
    all_to_all x3, starting transfers between devices, on_device(): lax.all_to_all(for_sending(stacked), 'ctx', split_axis=2, concat_axis=0,...  16.6 us
    all_to_all x3, waiting for transfers between devices, on_device(): lax.all_to_all(for_sending(stacked), 'ctx', split_axis=2, concat_axis=0,...  14.7 us
    slice x2, local copies, waits for them, and re-layouts, sent_together(): piece = whole[..., at:at + column.shape[along]]  6.41 us
    all_to_all x1, starting transfers between devices, sent_to_all(): return lax.all_to_all(copies, axis, split_axis=0, concat_axis=0, tiled=True)  6.33 us
  transfers between devices with their start and end apart: 5, of which 5 were waited for; matrix products, arithmetic and copies ran while one was open for 6% of the time, Pallas kernels for 0%

commit v1 on v0

--- a/solution.py
+++ b/solution.py
@@ -168,7 +168,15 @@
     head_values = head_values.reshape(seq_dev, node_block, -1)
     projected = jnp.einsum(
         "ksnv,vd->ksnd",
-        lax.all_gather(head_values[None], ("ctx", "dec"), axis=0, tiled=True),
+        jnp.concatenate(
+            lax.all_to_all(
+                jnp.stack([head_values[None]] * lax.axis_size(("ctx", "dec"))),
+                axis_name=("ctx", "dec"),
+                split_axis=0,
+                concat_axis=0,
+            ),
+            0,
+        ),
         out_proj,
         preferred_element_type=jnp.float32,
     )

time: 291 us -> 186 us (0.64)
  waiting for transfers between devices: 158 us -> 32.2 us
  blocking collectives: 30.2 us -> 66.7 us
  between operations: 14.5 us -> 1.15 us
    all_gather x1 -> x0, waiting for transfers between devices: 126 us -> none  [on_device(): lax.all_gather(head_values[None], ('ctx', 'dec'), axis=0, tiled=True)]
    all_to_all x0 -> x1, blocking collectives: none -> 50.4 us  [on_device(): lax.all_to_all(jnp.stack([head_values[None]] * lax.axis_size(('ctx', 'dec...]
    all_to_all x1, blocking collectives: 30.2 us -> 16.3 us  [sent_and_summed(): blocks = lax.all_to_all(in_blocks(value, dim, size), axis, 0, 0, tiled=True)]
    unnamed x31 -> x34, local copies, waits for them, and re-layouts: 18.9 us -> 18.9 us
  transfers between devices with their start and end apart: 5 -> 4, of which waited for: 5 -> 4; matrix products, arithmetic and copies ran while one was open for 6% -> 9% of each run, Pallas kernels for 0% -> 0%
where the time goes in v1:
time: 186 us; the launch traced here: 185 us
  blocking collectives  66.7 us (36%)
  local copies, waits for them, and re-layouts  38.3 us (21%)
  waiting for transfers between devices  32.2 us (17%)
  starting transfers between devices  22.9 us (12%)
  other arithmetic  12 us (6%)
  matrix products  11.4 us (6%)
    all_to_all x1, blocking collectives, on_device(): lax.all_to_all(jnp.stack([head_values[None]] * lax.axis_size(('ctx', 'dec...  50.4 us
    unnamed x34, local copies, waits for them, and re-layouts  18.9 us
    all_to_all x1, waiting for transfers between devices, sent_to_all(): return lax.all_to_all(copies, axis, split_axis=0, concat_axis=0, tiled=True)  17.5 us
    all_to_all x3, starting transfers between devices, on_device(): lax.all_to_all(for_sending(stacked), 'ctx', split_axis=2, concat_axis=0,...  16.6 us
    all_to_all x1, blocking collectives, sent_and_summed(): blocks = lax.all_to_all(in_blocks(value, dim, size), axis, 0, 0, tiled=True)  16.3 us
    all_to_all x3, waiting for transfers between devices, on_device(): lax.all_to_all(for_sending(stacked), 'ctx', split_axis=2, concat_axis=0,...  14.7 us
    slice x2, local copies, waits for them, and re-layouts, sent_together(): piece = whole[..., at:at + column.shape[along]]  6.41 us
    all_to_all x1, starting transfers between devices, sent_to_all(): return lax.all_to_all(copies, axis, split_axis=0, concat_axis=0, tiled=True)  6.33 us
  transfers between devices with their start and end apart: 4, of which 4 were waited for; matrix products, arithmetic and copies ran while one was open for 9% of the time, Pallas kernels for 0%

profile of v1, /device:TPU:1, one launch (start us, length us, event | category | flops | bytes accessed | tf_op | source)
XLA Modules:
  0.0 184.7 jit_solution(476925457785280670)
XLA Ops:
  0.8 1.0 maximum_bitcast_fusion
  1.8 1.6 broadcast_in_dim.58
  3.4 6.3 %all-to-all-start = ((bf16[8,1,256,577]{2,3,1,0:T(8,128)(2,1)}), bf16[8,1,256,577]{2,3,1,0:T(8,128)(2,1)}, u32[]{:S(2)}, u32[]{:S(2)}) async-start(bf16[8,1,256,577]{2,3,1,0:T(8,128)(2,1)} %broadcast_in_dim.58), calls=%async_computation | async-start | bytes 4784128 | tf_op jit(solution)/shard_map/all_to_all | solution.py:16
  10.0 0.2 convolution_minimum_fusion.5
  11.0 0.2 fusion.44
  11.2 1.4 fusion
  12.7 0.9 fusion.42
  13.6 0.7 copy.129
  14.2 1.7 fusion.23
  16.0 1.4 copy.136
  17.3 1.3 dynamic_slice.7
  18.6 1.2 bitcast_convert_fusion
  19.8 1.2 fusion.2
  21.0 0.2 fusion.26
  21.2 17.5 %all-to-all-done = bf16[8,1,256,577]{2,3,1,0:T(8,128)(2,1)} async-done(((bf16[8,1,256,577]{2,3,1,0:T(8,128)(2,1)}), bf16[8,1,256,577]{2,3,1,0:T(8,128)(2,1)}, u32[]{:S(2)}, u32[]{:S(2)}) %all-to-all-start) | async-done | bytes 2363424 | tf_op jit(solution)/shard_map/all_to_all | solution.py:16
  38.7 2.2 %copy.167 = bf16[8,1,256,577]{2,0,3,1:T(8,128)(2,1)S(1)} copy(bf16[8,1,256,577]{2,3,1,0:T(8,128)(2,1)} %all-to-all-done) | data formatting | bytes 4726784 | tf_op jit(solution)/shard_map/all_to_all | solution.py:16
  40.8 0.7 fusion.35
  41.6 1.6 slice.17
  43.2 4.8 %copy.118 = bf16[8,256,576]{2,1,0:T(8,128)(2,1)} copy(bf16[8,256,576]{1,0,2:T(8,128)(2,1)} %slice.17) | data formatting | bytes 4718592 | tf_op jit(solution)/shard_map/slice | solution.py:28
  48.0 5.8 %reshape.535 = bf16[1179648]{0:T(1024)(128)(2,1)} reshape(bf16[8,256,576]{2,1,0:T(8,128)(2,1)} %copy.118) | data formatting | bytes 4718592
  53.8 4.1 %reshape.517 = bf16[8,147456]{1,0:T(8,128)(2,1)} reshape(bf16[1179648]{0:T(1024)(128)(2,1)} %reshape.535) | data formatting | bytes 4718592 | tf_op jit(solution)/shard_map/reshape | solution.py:94
  57.9 4.2 %reshape.537 = bf16[1179648]{0:T(1024)(128)(2,1)} reshape(bf16[8,147456]{1,0:T(8,128)(2,1)} %reshape.517) | data formatting | bytes 4718592
  62.1 5.5 %reshape.538 = bf16[8,256,576]{2,1,0:T(8,128)(2,1)} reshape(bf16[1179648]{0:T(1024)(128)(2,1)} %reshape.537) | data formatting | bytes 4718592
  67.6 2.5 %multiply_reduce_fusion = bf16[256,576]{1,0:T(8,128)(2,1)S(1)} fusion(f32[8]{0:T(128)S(1)} %copy-done.10, bf16[8,256,576]{2,1,0:T(8,128)(2,1)} %reshape.538), kind=kLoop, calls=%fused_computation | loop fusion | flops 3391488 | bytes 2654240 | tf_op jit(solution)/shard_map/dot_general | solution.py:95
  70.1 2.0 %fusion.43 = (f32[64,16]{1,0:T(8,128)S(1)}, f32[64,16,256]{2,1,0:T(8,128)}) fusion(bf16[256,576]{1,0:T(8,128)(2,1)S(1)} %multiply_reduce_fusion, bf16[64,16,576]{2,0,1:T(8,128)(2,1)S(1)} %copy-done.2, pred[256]{0:T(512)(128)(4,1)S(1)} %convert_compare_fusion), kind=kOutput, calls=%fused_computation.80 | convolution fusion | flops 302775296 | bytes 2527488 | tf_op jit(solution)/shard_map/snhc,spc->snhp/dot_general | solution.py:67
  72.1 1.6 fusion.12
  73.8 0.6 broadcast.168
  74.4 0.8 reduce.17
  75.2 0.7 reshape.539
  75.9 7.7 %all-to-all-start.2 = ((bf16[4,2,128]{2,1,0:T(2,128)(2,1)}), bf16[4,2,128]{2,1,0:T(2,128)(2,1)S(1)}, u32[]{:S(2)}, u32[]{:S(2)}) async-start(bf16[4,2,128]{2,1,0:T(2,128)(2,1)} %reshape.539), calls=%async_computation.2 | async-start | bytes 4096 | tf_op jit(solution)/shard_map/all_to_all | solution.py:150
  83.6 0.4 fusion.15
  84.0 1.1 copy-done.1
  85.1 1.3 fusion.5
  86.6 0.8 reduce.18
  87.4 0.7 reshape.541
  88.1 0.9 copy.122
  88.9 1.1 all-to-all-done.2
  90.1 5.5 %all-to-all-start.3 = ((bf16[4,2,128]{2,1,0:T(2,128)(2,1)}), bf16[4,2,128]{2,1,0:T(2,128)(2,1)S(1)}, u32[]{:S(2)}, u32[]{:S(2)}) async-start(bf16[4,2,128]{2,1,0:T(2,128)(2,1)} %reshape.541), calls=%async_computation.3 | async-start | bytes 4096 | tf_op jit(solution)/shard_map/all_to_all | solution.py:150
  95.9 6.0 %all-to-all-done.3 = bf16[4,2,128]{2,1,0:T(2,128)(2,1)S(1)} async-done(((bf16[4,2,128]{2,1,0:T(2,128)(2,1)}), bf16[4,2,128]{2,1,0:T(2,128)(2,1)S(1)}, u32[]{:S(2)}, u32[]{:S(2)}) %all-to-all-start.3) | async-done | bytes 2080 | tf_op jit(solution)/shard_map/all_to_all | solution.py:150
  102.0 3.4 %all-to-all-start.1 = ((bf16[1,1,64,16,128]{4,3,1,0,2:T(8,128)(2,1)}), bf16[1,1,64,16,128]{4,3,1,0,2:T(8,128)(2,1)S(1)}, u32[]{:S(2)}, u32[]{:S(2)}) async-start(bf16[1,1,64,16,128]{4,3,1,0,2:T(8,128)(2,1)} %copy.122), calls=%async_computation.1 | async-start | bytes 524288 | tf_op jit(solution)/shard_map/all_to_all | solution.py:150
  105.8 7.6 %all-to-all-done.1 = bf16[1,1,64,16,128]{4,3,1,0,2:T(8,128)(2,1)S(1)} async-done(((bf16[1,1,64,16,128]{4,3,1,0,2:T(8,128)(2,1)}), bf16[1,1,64,16,128]{4,3,1,0,2:T(8,128)(2,1)S(1)}, u32[]{:S(2)}, u32[]{:S(2)}) %all-to-all-start.1) | async-done | bytes 262176 | tf_op jit(solution)/shard_map/all_to_all | solution.py:150
  113.4 0.2 fusion.14
  113.6 2.5 %fusion.10 = bf16[1,16,16,128]{3,1,2,0:T(8,128)(2,1)S(1)} fusion(f32[16,16,512]{2,0,1:T(8,128)S(1)} %fusion.26, bf16[16,512,128]{2,1,0:T(8,128)(2,1)} %param.18, f32[16,16,128]{2,1,0:T(8,128)S(1)} %fusion.14, f32[16,16]{0,1:T(8,128)S(1)} %get-tuple-element.5, f32[16,16]{0,1:T(8,128)S(1)} %get-tuple-element.7, f32[16,16]{0,1:T(8,128)S(1)} %get-tuple-element.6), kind=kOutput, calls=%fused_computation.21 | convolution fusion | flops 201490432 | bytes 2821120 | tf_op jit(solution)/shard_map/snhc,hcv->snhv/dot_general | solution.py:100
  116.2 0.2 stack.3
  116.4 50.4 %all_to_all.45 = bf16[32,1,1,16,2048]{4,3,2,1,0:T(8,128)(2,1)S(1)} all-to-all(bf16[32,1,1,16,2048]{4,3,2,1,0:T(8,128)(2,1)S(1)} %stack.3), channel_id=1, replica_groups=mesh['ctx'=4,'tp'=8,'dec'=8] {'ctx','dec'}, dimensions={0} | all-to-all | bytes 4194304 | tf_op jit(solution)/shard_map/all_to_all | solution.py:172
  166.8 0.8 fusion.4
  167.7 16.3 %all_to_all.46 = bf16[8,8,8,224]{3,2,1,0:T(8,128)(2,1)S(1)} all-to-all(bf16[8,8,8,224]{3,2,1,0:T(8,128)(2,1)S(1)} %copy.139), channel_id=1, replica_groups=mesh['ctx'=4,'tp'=8,'dec'=8] {'tp'}, dimensions={0} | all-to-all | bytes 458752 | tf_op jit(solution)/shard_map/all_to_all | solution.py:49
  184.0 0.7 reduce_sum.55
  (56 shorter events, 2.3 us)
Async XLA Ops:
  0.0 11.2 %copy-start = (bf16[16,128,512]{2,1,0:T(8,128)(2,1)S(1)}, bf16[16,128,512]{2,1,0:T(8,128)(2,1)}, u32[]{:S(2)}) copy-start(bf16[16,128,512]{2,1,0:T(8,128)(2,1)} %param.17) | copy-start | bytes 6291460
  3.4 6.3 %copy-start.3 = (bf16[1,64,16,64]{3,2,1,0:T(8,128)(2,1)S(1)}, bf16[1,64,16,64]{3,2,1,0:T(8,128)(2,1)}, u32[]{:S(2)}) copy-start(bf16[1,64,16,64]{3,2,1,0:T(8,128)(2,1)} %param.15) | copy-start | bytes 393220
  3.4 6.4 %copy-start.9 = (s32[1,64]{1,0:T(1,128)S(1)}, s32[1,64]{1,0:T(1,128)}, u32[]{:S(2)}) copy-start(s32[1,64]{1,0:T(1,128)} %param.13) | copy-start | bytes 772
  3.4 35.3 %all-to-all-start = ((bf16[8,1,256,577]{2,3,1,0:T(8,128)(2,1)}), bf16[8,1,256,577]{2,3,1,0:T(8,128)(2,1)}, u32[]{:S(2)}, u32[]{:S(2)}) async-start(bf16[8,1,256,577]{2,3,1,0:T(8,128)(2,1)} %broadcast_in_dim.58), calls=%async_computation | async-start | bytes 4784128 | tf_op jit(solution)/shard_map/all_to_all | solution.py:16
  11.2 1.5 copy-start.8
  11.2 1.5 copy-start.4
  13.6 0.7 copy-start.7
  62.1 5.5 %copy-start.10 = (f32[8]{0:T(128)S(1)}, f32[8]{0:T(128)}, u32[]{:S(2)}) copy-start(f32[8]{0:T(128)} %bitcast_convert_fusion) | copy-start | bytes 100
  67.6 2.5 %copy-start.2 = (bf16[64,16,576]{2,0,1:T(8,128)(2,1)S(1)}, bf16[64,16,576]{2,0,1:T(8,128)(2,1)}, u32[]{:S(2)}) copy-start(bf16[64,16,576]{2,0,1:T(8,128)(2,1)} %fusion.2) | copy-start | bytes 3538948
  75.9 14.2 %all-to-all-start.2 = ((bf16[4,2,128]{2,1,0:T(2,128)(2,1)}), bf16[4,2,128]{2,1,0:T(2,128)(2,1)S(1)}, u32[]{:S(2)}, u32[]{:S(2)}) async-start(bf16[4,2,128]{2,1,0:T(2,128)(2,1)} %reshape.539), calls=%async_computation.2 | async-start | bytes 4096 | tf_op jit(solution)/shard_map/all_to_all | solution.py:150
  83.6 1.6 copy-start.1
  85.1 20.6 %copy-start.5 = (f32[16,16]{0,1:T(8,128)S(1)}, f32[16,16]{0,1:T(8,128)}, u32[]{:S(2)}) copy-start(f32[16,16]{0,1:T(8,128)} %copy.129) | copy-start | bytes 3076
  85.1 20.6 %copy-start.6 = (f32[16,16]{0,1:T(8,128)S(1)}, f32[16,16]{0,1:T(8,128)}, u32[]{:S(2)}) copy-start(f32[16,16]{0,1:T(8,128)} %copy.136) | copy-start | bytes 3076
  90.1 11.9 %all-to-all-start.3 = ((bf16[4,2,128]{2,1,0:T(2,128)(2,1)}), bf16[4,2,128]{2,1,0:T(2,128)(2,1)S(1)}, u32[]{:S(2)}, u32[]{:S(2)}) async-start(bf16[4,2,128]{2,1,0:T(2,128)(2,1)} %reshape.541), calls=%async_computation.3 | async-start | bytes 4096 | tf_op jit(solution)/shard_map/all_to_all | solution.py:150
  102.0 11.4 %all-to-all-start.1 = ((bf16[1,1,64,16,128]{4,3,1,0,2:T(8,128)(2,1)}), bf16[1,1,64,16,128]{4,3,1,0,2:T(8,128)(2,1)S(1)}, u32[]{:S(2)}, u32[]{:S(2)}) async-start(bf16[1,1,64,16,128]{4,3,1,0,2:T(8,128)(2,1)} %copy.122), calls=%async_computation.1 | async-start | bytes 524288 | tf_op jit(solution)/shard_map/all_to_all | solution.py:150
  116.4 50.4 %copy-start.11 = (bf16[2048,224]{0,1:T(8,128)(2,1)S(1)}, bf16[2048,224]{0,1:T(8,128)(2,1)}, u32[]{:S(2)}) copy-start(bf16[2048,224]{0,1:T(8,128)(2,1)} %param.19) | copy-start | bytes 2752516
